TPU v7x, 512 devices: a whole 4x8x8 slice. The times are simulated.
512 devices in a mesh: group: 16 (over y, core), member: 32 (over x, z).
Axes of the slice: x: 4, y: 8, z: 8, core: 2. Of those that a mesh axis runs over, the one named last changes fastest.
Arguments:
- heads: bfloat16 [1048576, 768], P(('group', 'member')), may hold values from -16 to 16
- new_heads: bfloat16 [1024, 768], P('group'), may hold values from -16 to 16
- vectors: bfloat16 [512, 128, 768], P(('group', 'member')), may hold values from -16 to 16
- near_ids: int32 [512, 64], P(('group', 'member')), may hold values from 0 to 65535, as said below
Outputs:
- density: float32 [1024], P('group')
- spread: float32 [1024], P('group')
- reassign: float32 [512, 64, 128], P(('group', 'member'))
Inputs may be any that keep to these rules, and one draw needn't show every extreme that they name: `near_ids`: each row holds 64 different numbers; of one row at most 4 lie in one range j * 2048 to (j + 1) * 2048 - 1, and exactly 4 in some such range.
All inputs are finite; a program needn't handle non-finite values.
Results may differ from a plain program's by a relative error of at most 0.0003.
Values may be sent and summed in bfloat16 or wider, within the bound.
A program may use at most 64 MiB of HBM per device.

v0:
```python
import jax
import jax.numpy as jnp
from jax import lax
from jax.sharding import PartitionSpec as P


def passed_along(value, axis, steps):
    count = lax.axis_size(axis)
    pairs = [(source, (source + steps) % count) for source in range(count)]
    return lax.ppermute(value, axis, pairs)


def crowding(block, heads, head_sq, width):
    query_sq = jnp.sum(jnp.square(block.astype(jnp.float32)), axis=1)
    dots = lax.dot_general(
        block, heads, (((1,), (1,)), ((), ())), preferred_element_type=jnp.float32
    )
    excess = (query_sq[:, None] + head_sq[None, :] - 2.0 * dots) / width
    weight = 1.0 / jnp.square(1.0 + excess)
    return jnp.stack([jnp.sum(weight, axis=1), jnp.sum(weight * excess, axis=1)])


def distances(vec, rows, width):
    vec_sq = jnp.sum(jnp.square(vec.astype(jnp.float32)), axis=2)
    row_sq = jnp.sum(jnp.square(rows.astype(jnp.float32)), axis=2)
    dots = jnp.einsum("pbd,pkd->pkb", vec, rows, preferred_element_type=jnp.float32)
    return (row_sq[:, :, None] + vec_sq[:, None, :] - 2.0 * dots) / width


def per_device(heads, new_heads, vectors, near_ids):
    head_dev = heads.shape[0]
    width = heads.shape[1]
    groups = lax.axis_size("group")
    members = lax.axis_size("member")
    here = lax.axis_index("group")
    me = lax.axis_index("member")
    head_sq = jnp.sum(jnp.square(heads.astype(jnp.float32)), axis=1)
    new_count = new_heads.shape[0]
    table = jnp.zeros((groups, 2, new_count), jnp.float32)
    table = lax.dynamic_update_slice(
        table, crowding(new_heads, heads, head_sq, width)[None], (here, 0, 0)
    )

    def advance(step, carry):
        block, sums = carry
        block = passed_along(block, "group", 1)
        anchor = (here - step) % groups
        sums = lax.dynamic_update_slice(
            sums, crowding(block, heads, head_sq, width)[None], (anchor, 0, 0)
        )
        return (block, sums)

    unused, table = lax.fori_loop(1, groups, advance, (new_heads, table))
    mine = lax.psum_scatter(table, "group", scatter_dimension=0, tiled=True)
    mine = lax.psum(mine, "member")
    total_heads = float(head_dev * groups * members)
    density = jnp.log(mine[0, 0] / total_heads)
    spread = mine[0, 1] / mine[0, 0]
    lists = lax.all_gather(near_ids, "member", axis=0, tiled=True)
    blocks = lax.all_gather(vectors, "member", axis=0, tiled=True)
    owner = lists // head_dev
    local = lists % head_dev
    rows = jnp.take(heads, local, axis=0)
    rows, owned = (rows, owner == me)
    reassign = lax.psum_scatter(
        jnp.where(owned[:, :, None], distances(blocks, rows, width), 0.0),
        "member",
        scatter_dimension=0,
        tiled=True,
    )
    return (density, spread, reassign)


def solution(mesh):
    placed = (
        P(("group", "member"), None),
        P("group", None),
        P(("group", "member"), None, None),
        P(("group", "member"), None),
    )
    return jax.shard_map(
        per_device,
        mesh=mesh,
        in_specs=placed,
        out_specs=(P("group"), P("group"), P(("group", "member"), None, None)),
        check_vma=False,
    )
```

profile of v0, /device:TPU:32, one launch (start us, length us, event | category | flops | bytes accessed | tf_op | source)
XLA Modules:
  0.0 345.6 jit_solution(508991916548334194)
XLA Ops:
  8.2 44.1 %all-gather = s32[32,1,64]{2,1,0:T(1,128)S(1)} all-gather(s32[1,1,64]{2,1,0:T(1,128)} %bitcast.40), channel_id=1, replica_groups=mesh['group'=16,'member'=32] {'member'}, dimensions={0}, use_global_device_ids=true | all-gather | bytes 8448 | tf_op jit(solution)/shard_map/all_gather | solution.py:59
  52.4 1.3 dynamic-slice
  53.8 12.6 %gather_fusion = bf16[2048,768]{1,0:T(8,128)(2,1)} fusion(bf16[2048,768]{1,0:T(8,128)(2,1)} %param.6, s32[2048]{0:T(1024)S(1)} %broadcast_clamp_fusion), kind=kCustom, calls=%fused_computation | custom fusion | bytes 6299648 | tf_op jit(solution)/shard_map/jit(_take)/gather | solution.py:63
  69.0 1.3 multiply_reduce_fusion.3
  70.4 39.8 %all-gather.3.cloned.1.call-done = bf16[32,128,768]{2,1,0:T(8,128)(2,1)} async-done(((bf16[1,128,768]{2,1,0:T(8,128)(2,1)}), bf16[32,128,768]{2,1,0:T(8,128)(2,1)}) %all-gather.3.cloned.1.call-update) | async-done | bytes 6291472 | tf_op jit(solution)/shard_map/all_gather | solution.py:60
  110.2 4.2 %multiply_reduce_fusion.2 = f32[32,128]{1,0:T(8,128)S(1)} fusion(bf16[32,128,768]{2,1,0:T(8,128)(2,1)} %all-gather.3.cloned.1.call-done), kind=kLoop, calls=%fused_computation.9 | loop fusion | flops 9433088 | bytes 6307840 | tf_op jit(solution)/shard_map/reduce_sum | solution.py:24
  114.4 5.3 %fusion.9 = f32[32,64,128]{2,1,0:T(8,128)} fusion(bf16[32,128,768]{2,1,0:T(8,128)(2,1)} %all-gather.3.cloned.1.call-done, bf16[32,64,768]{2,1,0:T(8,128)(2,1)S(1)} %bitcast.36, pred[32,64]{1,0:T(8,128)(4,1)S(1)} %get-tuple-element.175, f32[32,128]{1,0:T(8,128)S(1)} %multiply_reduce_fusion.2, f32[32,64]{1,0:T(8,128)S(1)} %multiply_reduce_fusion.3, ...), kind=kOutput, calls=%fused_computation.21 | convolution fusion | flops 405536768 | bytes 10514432 | tf_op jit(solution)/shard_map/pbd,pkd->pkb/dot_general | solution.py:26
  119.8 99.5 %while.17 = (s32[]{:T(128)}, bf16[64,768]{1,0:T(8,128)(2,1)S(1)}, f32[16,2,64]{2,1,0:T(2,128)S(1)}, f32[2048]{0:T(1024)S(1)}, bf16[2048,768]{1,0:T(8,128)(2,1)S(...) while((s32[]{:T(128)}, bf16[64,768]{1,0:T(8,128)(2,1)S(1)}, ...), condition=%wide.region_8.9_spmd, body=%wide.region_4.8_spmd.sunk | while | flops 202784720 | bytes 3943724 | solution.py:53
  119.8 5.2 %collective-permute-done = bf16[64,768]{1,0:T(8,128)(2,1)S(1)} collective-permute-done((bf16[64,768]{1,0:T(8,128)(2,1)S(1)}, bf16[64,768]{1,0:T(8,128)(2,1)S(1)}, u32[]{:S(2)}, u32[]{:S(2)}) %collective-permute-start) | collective-permute-done | bytes 98336 | tf_op jit(solution)/shard_map/while/body/eval_jaxpr/ppermute | solution.py:10
  125.1 1.2 fusion.28
  126.4 5.2 %collective-permute-done = bf16[64,768]{1,0:T(8,128)(2,1)S(1)} collective-permute-done((bf16[64,768]{1,0:T(8,128)(2,1)S(1)}, bf16[64,768]{1,0:T(8,128)(2,1)S(1)}, u32[]{:S(2)}, u32[]{:S(2)}) %collective-permute-start) | collective-permute-done | bytes 98336 | tf_op jit(solution)/shard_map/while/body/eval_jaxpr/ppermute | solution.py:10
  133.1 5.2 %collective-permute-done = bf16[64,768]{1,0:T(8,128)(2,1)S(1)} collective-permute-done((bf16[64,768]{1,0:T(8,128)(2,1)S(1)}, bf16[64,768]{1,0:T(8,128)(2,1)S(1)}, u32[]{:S(2)}, u32[]{:S(2)}) %collective-permute-start) | collective-permute-done | bytes 98336 | tf_op jit(solution)/shard_map/while/body/eval_jaxpr/ppermute | solution.py:10
  138.4 1.2 fusion.28
  139.7 5.2 %collective-permute-done = bf16[64,768]{1,0:T(8,128)(2,1)S(1)} collective-permute-done((bf16[64,768]{1,0:T(8,128)(2,1)S(1)}, bf16[64,768]{1,0:T(8,128)(2,1)S(1)}, u32[]{:S(2)}, u32[]{:S(2)}) %collective-permute-start) | collective-permute-done | bytes 98336 | tf_op jit(solution)/shard_map/while/body/eval_jaxpr/ppermute | solution.py:10
  145.0 1.2 fusion.28
  146.3 5.2 %collective-permute-done = bf16[64,768]{1,0:T(8,128)(2,1)S(1)} collective-permute-done((bf16[64,768]{1,0:T(8,128)(2,1)S(1)}, bf16[64,768]{1,0:T(8,128)(2,1)S(1)}, u32[]{:S(2)}, u32[]{:S(2)}) %collective-permute-start) | collective-permute-done | bytes 98336 | tf_op jit(solution)/shard_map/while/body/eval_jaxpr/ppermute | solution.py:10
  153.0 5.2 %collective-permute-done = bf16[64,768]{1,0:T(8,128)(2,1)S(1)} collective-permute-done((bf16[64,768]{1,0:T(8,128)(2,1)S(1)}, bf16[64,768]{1,0:T(8,128)(2,1)S(1)}, u32[]{:S(2)}, u32[]{:S(2)}) %collective-permute-start) | collective-permute-done | bytes 98336 | tf_op jit(solution)/shard_map/while/body/eval_jaxpr/ppermute | solution.py:10
  158.3 1.2 fusion.28
  159.6 5.2 %collective-permute-done = bf16[64,768]{1,0:T(8,128)(2,1)S(1)} collective-permute-done((bf16[64,768]{1,0:T(8,128)(2,1)S(1)}, bf16[64,768]{1,0:T(8,128)(2,1)S(1)}, u32[]{:S(2)}, u32[]{:S(2)}) %collective-permute-start) | collective-permute-done | bytes 98336 | tf_op jit(solution)/shard_map/while/body/eval_jaxpr/ppermute | solution.py:10
  164.9 1.2 fusion.28
  166.2 5.2 %collective-permute-done = bf16[64,768]{1,0:T(8,128)(2,1)S(1)} collective-permute-done((bf16[64,768]{1,0:T(8,128)(2,1)S(1)}, bf16[64,768]{1,0:T(8,128)(2,1)S(1)}, u32[]{:S(2)}, u32[]{:S(2)}) %collective-permute-start) | collective-permute-done | bytes 98336 | tf_op jit(solution)/shard_map/while/body/eval_jaxpr/ppermute | solution.py:10
  172.9 5.2 %collective-permute-done = bf16[64,768]{1,0:T(8,128)(2,1)S(1)} collective-permute-done((bf16[64,768]{1,0:T(8,128)(2,1)S(1)}, bf16[64,768]{1,0:T(8,128)(2,1)S(1)}, u32[]{:S(2)}, u32[]{:S(2)}) %collective-permute-start) | collective-permute-done | bytes 98336 | tf_op jit(solution)/shard_map/while/body/eval_jaxpr/ppermute | solution.py:10
  179.5 5.2 %collective-permute-done = bf16[64,768]{1,0:T(8,128)(2,1)S(1)} collective-permute-done((bf16[64,768]{1,0:T(8,128)(2,1)S(1)}, bf16[64,768]{1,0:T(8,128)(2,1)S(1)}, u32[]{:S(2)}, u32[]{:S(2)}) %collective-permute-start) | collective-permute-done | bytes 98336 | tf_op jit(solution)/shard_map/while/body/eval_jaxpr/ppermute | solution.py:10
  184.8 1.2 fusion.28
  186.1 5.2 %collective-permute-done = bf16[64,768]{1,0:T(8,128)(2,1)S(1)} collective-permute-done((bf16[64,768]{1,0:T(8,128)(2,1)S(1)}, bf16[64,768]{1,0:T(8,128)(2,1)S(1)}, u32[]{:S(2)}, u32[]{:S(2)}) %collective-permute-start) | collective-permute-done | bytes 98336 | tf_op jit(solution)/shard_map/while/body/eval_jaxpr/ppermute | solution.py:10
  192.8 5.2 %collective-permute-done = bf16[64,768]{1,0:T(8,128)(2,1)S(1)} collective-permute-done((bf16[64,768]{1,0:T(8,128)(2,1)S(1)}, bf16[64,768]{1,0:T(8,128)(2,1)S(1)}, u32[]{:S(2)}, u32[]{:S(2)}) %collective-permute-start) | collective-permute-done | bytes 98336 | tf_op jit(solution)/shard_map/while/body/eval_jaxpr/ppermute | solution.py:10
  199.4 5.2 %collective-permute-done = bf16[64,768]{1,0:T(8,128)(2,1)S(1)} collective-permute-done((bf16[64,768]{1,0:T(8,128)(2,1)S(1)}, bf16[64,768]{1,0:T(8,128)(2,1)S(1)}, u32[]{:S(2)}, u32[]{:S(2)}) %collective-permute-start) | collective-permute-done | bytes 98336 | tf_op jit(solution)/shard_map/while/body/eval_jaxpr/ppermute | solution.py:10
  204.7 1.2 fusion.28
  206.0 5.2 %collective-permute-done = bf16[64,768]{1,0:T(8,128)(2,1)S(1)} collective-permute-done((bf16[64,768]{1,0:T(8,128)(2,1)S(1)}, bf16[64,768]{1,0:T(8,128)(2,1)S(1)}, u32[]{:S(2)}, u32[]{:S(2)}) %collective-permute-start) | collective-permute-done | bytes 98336 | tf_op jit(solution)/shard_map/while/body/eval_jaxpr/ppermute | solution.py:10
  212.7 5.2 %collective-permute-done = bf16[64,768]{1,0:T(8,128)(2,1)S(1)} collective-permute-done((bf16[64,768]{1,0:T(8,128)(2,1)S(1)}, bf16[64,768]{1,0:T(8,128)(2,1)S(1)}, u32[]{:S(2)}, u32[]{:S(2)}) %collective-permute-start) | collective-permute-done | bytes 98336 | tf_op jit(solution)/shard_map/while/body/eval_jaxpr/ppermute | solution.py:10
  219.3 46.5 %all-reduce = f32[16,2,64]{2,1,0:T(2,128)S(1)} all-reduce(f32[16,2,64]{2,1,0:T(2,128)S(1)} %get-tuple-element.158), channel_id=2, replica_groups=mesh['group'=16,'member'=32] {'group'}, use_global_device_ids=true, to_apply=%region_9.10.clone | all-reduce | flops 2048 | bytes 16384
  266.4 71.8 %psum.7 = f32[1,2,64]{2,1,0:T(2,128)S(1)} all-reduce(f32[1,2,64]{2,1,0:T(2,128)S(1)} %constant_dynamic-slice_fusion), channel_id=1, replica_groups=mesh['group'=16,'member'=32] {'member'}, use_global_device_ids=true, to_apply=%region_10.11 | all-reduce | flops 128 | bytes 1024 | tf_op jit(solution)/shard_map/psum | solution.py:55
  (90 shorter events, 17.0 us)
Async XLA Ops:
  7.2 103.0 %all-gather.3.cloned.1.call-start = ((), (), s32[]{:S(2)}) async-start(), calls=%async_computation.1 | async-start | bytes 6488064 | tf_op jit(solution)/shard_map/all_gather | solution.py:60
  8.1 330.6 %reduce-scatter.2.cloned.1.call-start = ((), (), s32[]{:S(2)}) async-start(), calls=%async_computation.2 | async-start | bytes 1081344 | tf_op jit(solution)/shard_map/reduce_scatter | solution.py:65
  53.8 12.7 %copy-start = (bf16[2048,768]{1,0:T(8,128)(2,1)S(1)}, bf16[2048,768]{1,0:T(8,128)(2,1)}, u32[]{:S(2)}) copy-start(bf16[2048,768]{1,0:T(8,128)(2,1)} %param.6) | copy-start | bytes 9437188
  67.1 1.9 copy-start.1
  110.2 4.2 %copy-start.2 = (bf16[2048,768]{1,0:T(8,128)(2,1)S(1)}, bf16[2048,768]{1,0:T(8,128)(2,1)}, u32[]{:S(2)}) copy-start(bf16[2048,768]{1,0:T(8,128)(2,1)} %gather_fusion) | copy-start | bytes 9437188
  119.8 5.3 %collective-permute-start = (bf16[64,768]{1,0:T(8,128)(2,1)S(1)}, bf16[64,768]{1,0:T(8,128)(2,1)S(1)}, u32[]{:S(2)}, u32[]{:S(2)}) collective-permute-start(bf16[64,768]{1,0:T(8,128)(2,1)S(1)} %get-tuple-element.232), channel_id=1, source_target_pairs={{0,32},{32,64},{64,96},{96,128},{128,160},{160,192},{192,224},{224... | collective-permute-start | bytes 294920 | tf_op jit(solution)/shard_map/while/body/eval_jaxpr/ppermute | solution.py:10
  126.4 5.3 %collective-permute-start = (bf16[64,768]{1,0:T(8,128)(2,1)S(1)}, bf16[64,768]{1,0:T(8,128)(2,1)S(1)}, u32[]{:S(2)}, u32[]{:S(2)}) collective-permute-start(bf16[64,768]{1,0:T(8,128)(2,1)S(1)} %get-tuple-element.232), channel_id=1, source_target_pairs={{0,32},{32,64},{64,96},{96,128},{128,160},{160,192},{192,224},{224... | collective-permute-start | bytes 294920 | tf_op jit(solution)/shard_map/while/body/eval_jaxpr/ppermute | solution.py:10
  133.0 5.3 %collective-permute-start = (bf16[64,768]{1,0:T(8,128)(2,1)S(1)}, bf16[64,768]{1,0:T(8,128)(2,1)S(1)}, u32[]{:S(2)}, u32[]{:S(2)}) collective-permute-start(bf16[64,768]{1,0:T(8,128)(2,1)S(1)} %get-tuple-element.232), channel_id=1, source_target_pairs={{0,32},{32,64},{64,96},{96,128},{128,160},{160,192},{192,224},{224... | collective-permute-start | bytes 294920 | tf_op jit(solution)/shard_map/while/body/eval_jaxpr/ppermute | solution.py:10
  139.7 5.3 %collective-permute-start = (bf16[64,768]{1,0:T(8,128)(2,1)S(1)}, bf16[64,768]{1,0:T(8,128)(2,1)S(1)}, u32[]{:S(2)}, u32[]{:S(2)}) collective-permute-start(bf16[64,768]{1,0:T(8,128)(2,1)S(1)} %get-tuple-element.232), channel_id=1, source_target_pairs={{0,32},{32,64},{64,96},{96,128},{128,160},{160,192},{192,224},{224... | collective-permute-start | bytes 294920 | tf_op jit(solution)/shard_map/while/body/eval_jaxpr/ppermute | solution.py:10
  146.3 5.3 %collective-permute-start = (bf16[64,768]{1,0:T(8,128)(2,1)S(1)}, bf16[64,768]{1,0:T(8,128)(2,1)S(1)}, u32[]{:S(2)}, u32[]{:S(2)}) collective-permute-start(bf16[64,768]{1,0:T(8,128)(2,1)S(1)} %get-tuple-element.232), channel_id=1, source_target_pairs={{0,32},{32,64},{64,96},{96,128},{128,160},{160,192},{192,224},{224... | collective-permute-start | bytes 294920 | tf_op jit(solution)/shard_map/while/body/eval_jaxpr/ppermute | solution.py:10
  152.9 5.3 %collective-permute-start = (bf16[64,768]{1,0:T(8,128)(2,1)S(1)}, bf16[64,768]{1,0:T(8,128)(2,1)S(1)}, u32[]{:S(2)}, u32[]{:S(2)}) collective-permute-start(bf16[64,768]{1,0:T(8,128)(2,1)S(1)} %get-tuple-element.232), channel_id=1, source_target_pairs={{0,32},{32,64},{64,96},{96,128},{128,160},{160,192},{192,224},{224... | collective-permute-start | bytes 294920 | tf_op jit(solution)/shard_map/while/body/eval_jaxpr/ppermute | solution.py:10
  159.6 5.3 %collective-permute-start = (bf16[64,768]{1,0:T(8,128)(2,1)S(1)}, bf16[64,768]{1,0:T(8,128)(2,1)S(1)}, u32[]{:S(2)}, u32[]{:S(2)}) collective-permute-start(bf16[64,768]{1,0:T(8,128)(2,1)S(1)} %get-tuple-element.232), channel_id=1, source_target_pairs={{0,32},{32,64},{64,96},{96,128},{128,160},{160,192},{192,224},{224... | collective-permute-start | bytes 294920 | tf_op jit(solution)/shard_map/while/body/eval_jaxpr/ppermute | solution.py:10
  166.2 5.3 %collective-permute-start = (bf16[64,768]{1,0:T(8,128)(2,1)S(1)}, bf16[64,768]{1,0:T(8,128)(2,1)S(1)}, u32[]{:S(2)}, u32[]{:S(2)}) collective-permute-start(bf16[64,768]{1,0:T(8,128)(2,1)S(1)} %get-tuple-element.232), channel_id=1, source_target_pairs={{0,32},{32,64},{64,96},{96,128},{128,160},{160,192},{192,224},{224... | collective-permute-start | bytes 294920 | tf_op jit(solution)/shard_map/while/body/eval_jaxpr/ppermute | solution.py:10
  172.8 5.3 %collective-permute-start = (bf16[64,768]{1,0:T(8,128)(2,1)S(1)}, bf16[64,768]{1,0:T(8,128)(2,1)S(1)}, u32[]{:S(2)}, u32[]{:S(2)}) collective-permute-start(bf16[64,768]{1,0:T(8,128)(2,1)S(1)} %get-tuple-element.232), channel_id=1, source_target_pairs={{0,32},{32,64},{64,96},{96,128},{128,160},{160,192},{192,224},{224... | collective-permute-start | bytes 294920 | tf_op jit(solution)/shard_map/while/body/eval_jaxpr/ppermute | solution.py:10
  179.5 5.3 %collective-permute-start = (bf16[64,768]{1,0:T(8,128)(2,1)S(1)}, bf16[64,768]{1,0:T(8,128)(2,1)S(1)}, u32[]{:S(2)}, u32[]{:S(2)}) collective-permute-start(bf16[64,768]{1,0:T(8,128)(2,1)S(1)} %get-tuple-element.232), channel_id=1, source_target_pairs={{0,32},{32,64},{64,96},{96,128},{128,160},{160,192},{192,224},{224... | collective-permute-start | bytes 294920 | tf_op jit(solution)/shard_map/while/body/eval_jaxpr/ppermute | solution.py:10
  186.1 5.3 %collective-permute-start = (bf16[64,768]{1,0:T(8,128)(2,1)S(1)}, bf16[64,768]{1,0:T(8,128)(2,1)S(1)}, u32[]{:S(2)}, u32[]{:S(2)}) collective-permute-start(bf16[64,768]{1,0:T(8,128)(2,1)S(1)} %get-tuple-element.232), channel_id=1, source_target_pairs={{0,32},{32,64},{64,96},{96,128},{128,160},{160,192},{192,224},{224... | collective-permute-start | bytes 294920 | tf_op jit(solution)/shard_map/while/body/eval_jaxpr/ppermute | solution.py:10
  192.7 5.3 %collective-permute-start = (bf16[64,768]{1,0:T(8,128)(2,1)S(1)}, bf16[64,768]{1,0:T(8,128)(2,1)S(1)}, u32[]{:S(2)}, u32[]{:S(2)}) collective-permute-start(bf16[64,768]{1,0:T(8,128)(2,1)S(1)} %get-tuple-element.232), channel_id=1, source_target_pairs={{0,32},{32,64},{64,96},{96,128},{128,160},{160,192},{192,224},{224... | collective-permute-start | bytes 294920 | tf_op jit(solution)/shard_map/while/body/eval_jaxpr/ppermute | solution.py:10
  199.4 5.3 %collective-permute-start = (bf16[64,768]{1,0:T(8,128)(2,1)S(1)}, bf16[64,768]{1,0:T(8,128)(2,1)S(1)}, u32[]{:S(2)}, u32[]{:S(2)}) collective-permute-start(bf16[64,768]{1,0:T(8,128)(2,1)S(1)} %get-tuple-element.232), channel_id=1, source_target_pairs={{0,32},{32,64},{64,96},{96,128},{128,160},{160,192},{192,224},{224... | collective-permute-start | bytes 294920 | tf_op jit(solution)/shard_map/while/body/eval_jaxpr/ppermute | solution.py:10
  206.0 5.3 %collective-permute-start = (bf16[64,768]{1,0:T(8,128)(2,1)S(1)}, bf16[64,768]{1,0:T(8,128)(2,1)S(1)}, u32[]{:S(2)}, u32[]{:S(2)}) collective-permute-start(bf16[64,768]{1,0:T(8,128)(2,1)S(1)} %get-tuple-element.232), channel_id=1, source_target_pairs={{0,32},{32,64},{64,96},{96,128},{128,160},{160,192},{192,224},{224... | collective-permute-start | bytes 294920 | tf_op jit(solution)/shard_map/while/body/eval_jaxpr/ppermute | solution.py:10
  212.6 5.3 %collective-permute-start = (bf16[64,768]{1,0:T(8,128)(2,1)S(1)}, bf16[64,768]{1,0:T(8,128)(2,1)S(1)}, u32[]{:S(2)}, u32[]{:S(2)}) collective-permute-start(bf16[64,768]{1,0:T(8,128)(2,1)S(1)} %get-tuple-element.232), channel_id=1, source_target_pairs={{0,32},{32,64},{64,96},{96,128},{128,160},{160,192},{192,224},{224... | collective-permute-start | bytes 294920 | tf_op jit(solution)/shard_map/while/body/eval_jaxpr/ppermute | solution.py:10
Sparse Core Ops, SparseCore 0:
  11.2 98.9 all-gather.2
  119.9 217.1 reduce-scatter.1
where the time goes:
time: 346 us
  blocking collectives  162 us (47%)
  waiting for transfers between devices  118 us (34%)
  matrix products  24.4 us (7%)
  local copies, waits for them, and re-layouts  16.3 us (5%)
  between operations  14.1 us (4%)
  other arithmetic  9.04 us (3%)
    ppermute x15, waiting for transfers between devices, passed_along(): return lax.ppermute(value, axis, pairs)  78.2 us
    psum x1, blocking collectives, per_device(): mine = lax.psum(mine, 'member')  71.8 us
    unnamed x1, blocking collectives  46.5 us
    all_gather x1, blocking collectives, per_device(): lists = lax.all_gather(near_ids, 'member', axis=0, tiled=True)  44.1 us
    all_gather x1, waiting for transfers between devices, per_device(): blocks = lax.all_gather(vectors, 'member', axis=0, tiled=True)  39.8 us
    dot_general x16, matrix products, crowding(): lax.dot_general(block, heads, (((1,), (1,)), ((), ())), preferred_element...  19.2 us
    gather x1, local copies, waits for them, and re-layouts, per_device(): rows = jnp.take(heads, local, axis=0)  12.6 us
  transfers between devices with their start and end apart: 17, of which 16 were waited for; matrix products, arithmetic and copies ran while one was open for 11% of the time, Pallas kernels for 0%

commit v1 on v0

v1 whole, which is shorter than its diff:
```python
import functools

import jax
import jax.numpy as jnp
from jax import lax
from jax.experimental import pallas as pl
from jax.experimental.pallas import tpu as pltpu
from jax.sharding import PartitionSpec as P

F32 = jnp.float32
BF16 = jnp.bfloat16
MOST = 4
NT = (((1,), (1,)), ((), ()))


def row_of(column):
    n = column.shape[0]
    return jnp.transpose(jnp.broadcast_to(column, (n, 128)))[0:1, :]


def kernel(
    shape,
    heads_hbm,
    new_ref,
    vec_ref,
    ids_ref,
    density_ref,
    spread_ref,
    reassign_ref,
    heads,
    half_sq,
    table,
    ids_all,
    row_out,
    row_in,
    part_out,
    part_in,
    sum_out,
    sum_in,
    heads_sem,
    own_sem,
    ring_send,
    ring_recv,
    twin_send,
    twin_recv,
    ids_send,
    ids_recv,
    row_send,
    row_recv,
    part_send,
    part_recv,
    sum_send,
    sum_recv,
):
    groups, members, total_heads = shape
    chips = groups // 2
    here = lax.axis_index("group")
    me = lax.axis_index("member")
    y = here // 2
    core = here % 2
    twin = y * 2 + (1 - core)
    head_dev, width = heads.shape
    block = new_ref.shape[0]
    near = ids_ref.shape[1]
    posts = vec_ref.shape[0]
    pair = 2 * block
    scale = width / 2.0

    def chip(step):
        return lax.rem(y + step + chips, chips)

    heads_copy = pltpu.make_async_copy(heads_hbm, heads, heads_sem)
    heads_copy.start()

    barrier = pltpu.get_barrier_semaphore()

    def greet_member(j, c):
        pl.semaphore_signal(
            barrier,
            inc=1,
            device_id=(here, lax.rem(me + j, members)),
            device_id_type=pl.DeviceIdType.MESH,
        )
        return c

    def greet_group(j, c):
        pl.semaphore_signal(
            barrier,
            inc=1,
            device_id=(lax.rem(here + j, groups), me),
            device_id_type=pl.DeviceIdType.MESH,
        )
        return c

    lax.fori_loop(1, members, greet_member, 0)
    lax.fori_loop(1, groups, greet_group, 0)
    pl.semaphore_wait(barrier, members - 1 + groups - 1)

    def remote(src, dst, send, recv, device):
        copy = pltpu.make_async_remote_copy(
            src_ref=src,
            dst_ref=dst,
            send_sem=send,
            recv_sem=recv,
            device_id=device,
            device_id_type=pl.DeviceIdType.MESH,
        )
        return copy

    last = chips // 2

    def base(step, way):
        if step == 0:
            return 0
        if step == last:
            return pair * (2 * last - 1)
        return pair * (1 + 2 * (step - 1) + way)

    def mine(step, way, which):
        start = pl.multiple_of(base(step, way) + which * block, block)
        if step == last:
            half = block // 2
            return table.at[pl.ds(pl.multiple_of(start + way * half, half), half)]
        return table.at[pl.ds(start, block)]

    def source(step, way):
        if step == 1:
            if step == last:
                return new_ref.at[pl.ds(way * (block // 2), block // 2)]
            return new_ref
        start = pl.multiple_of(base(step - 1, way) + core * block, block)
        if step == last:
            half = block // 2
            return table.at[pl.ds(pl.multiple_of(start + way * half, half), half)]
        return table.at[pl.ds(start, block)]

    def ring_copy(step, way):
        target = chip(1 if way == 0 else -1) * 2 + core
        return remote(
            source(step, way),
            mine(step, way, core),
            ring_send.at[step - 1, way],
            ring_recv.at[step - 1, way],
            (target, me),
        )

    def twin_copy(step, way):
        if step == 0:
            src = new_ref
        else:
            src = mine(step, way, core)
        return remote(
            src, mine(step, way, core), twin_send.at[step, way], twin_recv.at[step, way], (twin, me)
        )

    def twin_wait(step, way):
        pltpu.make_async_copy(
            mine(step, way, 1 - core), mine(step, way, 1 - core), twin_recv.at[step, way]
        ).wait()

    ring = {}
    for way in range(2):
        ring[1, way] = ring_copy(1, way)
        ring[1, way].start()
    twins = {(0, 0): twin_copy(0, 0)}
    twins[0, 0].start()
    own = pltpu.make_async_copy(new_ref, mine(0, 0, core), own_sem.at[0])
    own.start()

    ids_own = pltpu.make_async_copy(ids_ref, ids_all.at[me], ids_recv)
    ids_own.start()

    def send_ids(j, c):
        remote(
            ids_ref, ids_all.at[me], ids_send, ids_recv, (here, lax.rem(me + j, members))
        ).start()
        return c

    lax.fori_loop(1, members, send_ids, 0)

    heads_copy.wait()
    tile = 256

    def square(t, c):
        at = pl.ds(pl.multiple_of(t * tile, tile), tile)
        h = heads[at, :].astype(F32)
        half_sq[at, :] = jnp.broadcast_to(
            0.5 * jnp.sum(h * h, axis=1, keepdims=True), (tile, 128)
        )
        return c

    lax.fori_loop(0, head_dev // tile, square, 0)

    def crowding(start, count):
        blk = table[pl.ds(start, count), :]
        b32 = blk.astype(F32)
        query = row_of(0.5 * jnp.sum(b32 * b32, axis=1, keepdims=True))

        def step(t, carry):
            acc_w, acc_we = carry
            at = pl.ds(pl.multiple_of(t * tile, tile), tile)
            dots = lax.dot_general(heads[at, :], blk, NT, preferred_element_type=F32)
            hs = half_sq[at, :]
            if count > 128:
                hs = jnp.concatenate([hs] * (count // 128), axis=1)
            u = (hs + query) - dots
            r = 1.0 / (u + scale)
            w = r * r
            we = w * u
            acc_w += jnp.sum(w.reshape(tile // 8, 8, count), axis=0)
            acc_we += jnp.sum(we.reshape(tile // 8, 8, count), axis=0)
            return acc_w, acc_we

        zero = jnp.zeros((8, count), F32)
        acc_w, acc_we = lax.fori_loop(0, head_dev // tile, step, (zero, zero))
        w = (scale * scale) * jnp.sum(acc_w, axis=0, keepdims=True)
        we = scale * jnp.sum(acc_we, axis=0, keepdims=True)
        return w, we

    def send_parts(slot, step, w, we):
        part_out[slot] = jnp.concatenate([w, we], axis=1)
        if step == 0:
            pltpu.make_async_copy(part_out.at[slot], part_in.at[here], part_recv).start()
            remote(part_out.at[slot], part_in.at[here], part_send, part_recv, (twin, me)).start()
        else:
            for c in range(2):
                remote(
                    part_out.at[slot],
                    part_in.at[here],
                    part_send,
                    part_recv,
                    (chip(step) * 2 + c, me),
                ).start()

    def unit(step):
        if step == 0:
            own.wait()
            twin_wait(0, 0)
            w, we = crowding(0, pair)
            send_parts(0, 0, w, we)
        elif step == last:
            for way in range(2):
                twin_wait(step, way)
            w, we = crowding(base(step, 0), pair)
            send_parts(2 * last - 1, step, w, we)
        else:
            for way in range(2):
                twin_wait(step, way)
            w, we = crowding(base(step, 0), 2 * pair)
            for way in range(2):
                lanes = slice(way * pair, (way + 1) * pair)
                send_parts(
                    1 + 2 * (step - 1) + way,
                    -step if way == 0 else step,
                    w[:, lanes],
                    we[:, lanes],
                )

    def arrive(step):
        for way in range(2):
            ring[step, way].wait_recv()
            if step < last:
                ring[step + 1, way] = ring_copy(step + 1, way)
                ring[step + 1, way].start()
            twins[step, way] = twin_copy(step, way)
            twins[step, way].start()

    def pick_rows():
        pltpu.make_async_copy(ids_all, ids_all, ids_recv).wait()
        ids = ids_all[:, 0, :]
        owner = ids // head_dev
        local = (ids - owner * head_dev).astype(F32)
        held = owner == me
        before = (
            lax.broadcasted_iota(jnp.int32, (near, near), 0)
            < lax.broadcasted_iota(jnp.int32, (near, near), 1)
        ).astype(F32)
        rank = jnp.dot(
            held.astype(F32).astype(BF16), before.astype(BF16), preferred_element_type=F32
        )
        columns = []
        for r in range(MOST):
            hit = jnp.where(held & (rank == float(r)), local + 1.0, 0.0)
            columns.append(jnp.sum(hit, axis=1, keepdims=True) - 1.0)
        column = jnp.concatenate(columns, axis=0)
        slots = MOST * members
        picked = jnp.zeros((slots, width), F32)
        for t in range(head_dev // tile):
            lane = (lax.broadcasted_iota(jnp.int32, (slots, tile), 1) + t * tile).astype(F32)
            onehot = (lane == column).astype(F32).astype(BF16)
            picked += jnp.dot(
                onehot, heads[t * tile : (t + 1) * tile, :], preferred_element_type=F32
            )
        picked = picked.astype(BF16)
        cut = row_out.shape[2]
        place = lax.broadcasted_iota(jnp.int32, (members * 16, slots), 0)
        slot = lax.broadcasted_iota(jnp.int32, (members * 16, slots), 1)
        target = lax.rem(slot, members) * 16 + slot // members
        packed = jnp.zeros((members * 16, cut), F32)
        for c in range(width // cut):
            move = (place == target + MOST * c).astype(F32).astype(BF16)
            packed += jnp.dot(
                move, picked[:, c * cut : (c + 1) * cut], preferred_element_type=F32
            )
        row_out[...] = packed.astype(BF16).reshape(members, 16, cut)
        pltpu.make_async_copy(row_out.at[me], row_in.at[me], row_recv).start()

        def send(j, c):
            to = lax.rem(me + j, members)
            remote(row_out.at[to], row_in.at[me], row_send, row_recv, (here, to)).start()
            return c

        lax.fori_loop(1, members, send, 0)

    def finish_rows():
        pltpu.make_async_copy(row_in, row_in, row_recv).wait()
        cut = row_in.shape[2]
        owner = jnp.broadcast_to((ids_ref[...] // head_dev).astype(F32), (near, near))
        i = lax.broadcasted_iota(jnp.int32, (near, near), 0)
        j = lax.broadcasted_iota(jnp.int32, (near, near), 1)
        column = jnp.sum(jnp.where(i == j, owner, 0.0), axis=1, keepdims=True)
        rank = jnp.sum(
            jnp.where((owner == column) & (j < i), 1.0, 0.0), axis=1, keepdims=True
        )
        got = row_in[...].reshape(members * 16, cut)
        lane = lax.broadcasted_iota(jnp.int32, (near, members * 16), 1).astype(F32)
        want = column * 16.0 + rank
        dots = jnp.zeros((near, posts), F32)
        row_sq = jnp.zeros((near, 1), F32)
        vec_sq = jnp.zeros((posts, 1), F32)
        for c in range(width // cut):
            choose = (lane == want + float(MOST * c)).astype(F32).astype(BF16)
            rows = jnp.dot(choose, got, preferred_element_type=F32)
            vec = vec_ref[:, c * cut : (c + 1) * cut]
            v32 = vec.astype(F32)
            row_sq += jnp.sum(rows * rows, axis=1, keepdims=True)
            vec_sq += jnp.sum(v32 * v32, axis=1, keepdims=True)
            dots += lax.dot_general(rows.astype(BF16), vec, NT, preferred_element_type=F32)
        reassign_ref[...] = (row_sq + row_of(vec_sq) - 2.0 * dots) / width

    arrive(1)
    unit(0)
    pick_rows()
    for step in range(2, last + 1):
        arrive(step)
        unit(step - 1)
    unit(last)

    pltpu.make_async_copy(part_in, part_in, part_recv).wait()
    sum_out[...] = jnp.sum(part_in[...], axis=0)
    pltpu.make_async_copy(sum_out, sum_in.at[me], sum_recv).start()

    def send_sum(j, c):
        remote(sum_out, sum_in.at[me], sum_send, sum_recv, (here, lax.rem(me + j, members))).start()
        return c

    lax.fori_loop(1, members, send_sum, 0)
    finish_rows()
    pltpu.make_async_copy(sum_in, sum_in, sum_recv).wait()
    total = jnp.sum(sum_in[...], axis=0)
    w = total[:, 0:pair]
    we = total[:, pair : 2 * pair]
    w = jnp.where(core == 0, w[:, 0:block], w[:, block:pair])
    we = jnp.where(core == 0, we[:, 0:block], we[:, block:pair])
    density_ref[...] = jnp.log(w / float(total_heads))
    spread_ref[...] = we / w

    for copy in ring.values():
        copy.wait_send()
    for copy in twins.values():
        copy.wait_send()
    others = pl.ds(0, members - 1)
    pltpu.make_async_copy(ids_all.at[others], ids_all.at[others], ids_send).wait()
    pltpu.make_async_copy(row_in.at[others], row_in.at[others], row_send).wait()
    pltpu.make_async_copy(sum_in.at[others], sum_in.at[others], sum_send).wait()
    others = pl.ds(0, groups - 1)
    pltpu.make_async_copy(part_in.at[others], part_in.at[others], part_send).wait()


def per_device(heads, new_heads, vectors, near_ids):
    groups = lax.axis_size("group")
    members = lax.axis_size("member")
    head_dev, width = heads.shape
    block = new_heads.shape[0]
    posts = vectors.shape[1]
    near = near_ids.shape[1]
    last = groups // 4
    vmem = pl.BlockSpec(memory_space=pltpu.VMEM)
    dma = pltpu.SemaphoreType.DMA
    density, spread, reassign = pl.pallas_call(
        functools.partial(kernel, (groups, members, head_dev * groups * members)),
        out_shape=(
            jax.ShapeDtypeStruct((1, block), F32),
            jax.ShapeDtypeStruct((1, block), F32),
            jax.ShapeDtypeStruct((near, posts), F32),
        ),
        in_specs=[pl.BlockSpec(memory_space=pl.ANY), vmem, vmem, vmem],
        out_specs=(vmem, vmem, vmem),
        scratch_shapes=[
            pltpu.VMEM((head_dev, width), BF16),
            pltpu.VMEM((head_dev, 128), F32),
            pltpu.VMEM((groups * block, width), BF16),
            pltpu.VMEM((members, 1, near), jnp.int32),
            pltpu.VMEM((members, 16, 256), BF16),
            pltpu.VMEM((members, 16, 256), BF16),
            pltpu.VMEM((groups // 2, 1, 4 * block), F32),
            pltpu.VMEM((groups, 1, 4 * block), F32),
            pltpu.VMEM((1, 4 * block), F32),
            pltpu.VMEM((members, 1, 4 * block), F32),
            dma,
            dma((1,)),
            dma((last, 2)),
            dma((last, 2)),
            dma((last + 1, 2)),
            dma((last + 1, 2)),
            dma, dma, dma, dma, dma, dma, dma, dma,
        ],
        compiler_params=pltpu.CompilerParams(
            collective_id=0, has_side_effects=True, vmem_limit_bytes=40 * 1024 * 1024
        ),
    )(heads, new_heads, vectors[0], near_ids)
    return density[0], spread[0], reassign[None]


def solution(mesh):
    placed = (
        P(("group", "member"), None),
        P("group", None),
        P(("group", "member"), None, None),
        P(("group", "member"), None),
    )
    return jax.shard_map(
        per_device,
        mesh=mesh,
        in_specs=placed,
        out_specs=(P("group"), P("group"), P(("group", "member"), None, None)),
        check_vma=False,
    )
```

time: 346 us -> 54.8 us (0.16)
  the two profiles are of different devices: /device:TPU:32 before, /device:TPU:1 now
where the time goes in v1:
time: 54.8 us; the launch traced here: 54.5 us
  Pallas kernels  47.9 us (87%)
  local copies, waits for them, and re-layouts  5.99 us (11%)
  between operations  0.65 us (1%)
    pallas_call x1, Pallas kernels, per_device(): pl.pallas_call(functools.partial(kernel, (groups, members, head_dev * gro...  47.9 us
    unnamed x11, local copies, waits for them, and re-layouts  5.99 us

profile of v1, /device:TPU:1, one launch (start us, length us, event | category | flops | bytes accessed | tf_op | source)
XLA Modules:
  0.0 54.5 jit_solution(4452805340802457558)
XLA Ops:
  0.6 0.0 copy-start
  0.6 1.9 %copy-done = bf16[2048,768]{1,0:T(8,128)(2,1)S(1)} copy-done((bf16[2048,768]{1,0:T(8,128)(2,1)S(1)}, bf16[2048,768]{1,0:T(8,128)(2,1)}, u32[]{:S(2)}) %copy-start) | copy-done | bytes 3145752
  2.5 0.0 copy-start.1
  2.5 0.9 %copy-done.1 = bf16[1,128,768]{2,1,0:T(8,128)(2,1)S(1)} copy-done((bf16[1,128,768]{2,1,0:T(8,128)(2,1)S(1)}, bf16[1,128,768]{2,1,0:T(8,128)(2,1)}, u32[]{:S(2)}) %copy-start.1) | copy-done | bytes 196632
  3.4 0.0 copy-start.2
  3.5 0.9 %copy-done.2 = bf16[64,768]{1,0:T(8,128)(2,1)S(1)} copy-done((bf16[64,768]{1,0:T(8,128)(2,1)S(1)}, bf16[64,768]{1,0:T(8,128)(2,1)}, u32[]{:S(2)}) %copy-start.2) | copy-done | bytes 98328
  4.3 0.0 copy-start.3
  4.3 0.7 %copy-done.3 = s32[1,64]{1,0:T(1,128)S(1)} copy-done((s32[1,64]{1,0:T(1,128)S(1)}, s32[1,64]{1,0:T(1,128)}, u32[]{:S(2)}) %copy-start.3) | copy-done | bytes 280
  5.0 47.9 %shard_map.67 = (f32[1,64]{1,0:T(1,128)S(1)}, f32[1,64]{1,0:T(1,128)S(1)}, f32[64,128]{1,0:T(8,128)S(1)}) custom-call(bf16[2048,768]{1,0:T(8,128)(2,1)S(1)} %copy-done, bf16[64,768]{1,0:T(8,128)(2,1)S(1)} %copy-done.2, bf16[128,768]{1,0:T(8,128)(2,1)S(1)} %bitcast.4, s32[1,64]{1,0:T(1,128)S(1)} %copy-done.3), custom_call_target="tpu_custom_call" | custom-call | tf_op jit(solution)/shard_map/pallas_call | solution.py:390
  52.9 0.5 copy.10
  53.4 0.5 copy.11
  53.9 0.6 %copy.12 = f32[1,64,128]{2,1,0:T(8,128)} copy(f32[1,64,128]{2,1,0:T(8,128)S(1)} %bitcast.5) | data formatting | bytes 65536
Async XLA Ops:
  0.6 1.9 %copy-start = (bf16[2048,768]{1,0:T(8,128)(2,1)S(1)}, bf16[2048,768]{1,0:T(8,128)(2,1)}, u32[]{:S(2)}) copy-start(bf16[2048,768]{1,0:T(8,128)(2,1)} %heads_hbm.1) | copy-start | bytes 9437188
  2.5 0.9 %copy-start.1 = (bf16[1,128,768]{2,1,0:T(8,128)(2,1)S(1)}, bf16[1,128,768]{2,1,0:T(8,128)(2,1)}, u32[]{:S(2)}) copy-start(bf16[1,128,768]{2,1,0:T(8,128)(2,1)} %param.6) | copy-start | bytes 589828
  3.4 0.9 %copy-start.2 = (bf16[64,768]{1,0:T(8,128)(2,1)S(1)}, bf16[64,768]{1,0:T(8,128)(2,1)}, u32[]{:S(2)}) copy-start(bf16[64,768]{1,0:T(8,128)(2,1)} %new_ref.1) | copy-start | bytes 294916
  4.3 0.7 %copy-start.3 = (s32[1,64]{1,0:T(1,128)S(1)}, s32[1,64]{1,0:T(1,128)}, u32[]{:S(2)}) copy-start(s32[1,64]{1,0:T(1,128)} %ids_ref.1) | copy-start | bytes 772

commit v2 on v1

v2 whole, which is shorter than its diff:
```python
import functools

import jax
import jax.numpy as jnp
from jax import lax
from jax.experimental import pallas as pl
from jax.experimental.pallas import tpu as pltpu
from jax.sharding import PartitionSpec as P

F32 = jnp.float32
BF16 = jnp.bfloat16
MOST = 4
SHADES = 4
SLOTS = (0, -1, 1, -2, 2, -3, 3, 4)
ACROSS = 7
NT = (((1,), (1,)), ((), ()))


def row_of(column):
    n = column.shape[0]
    return jnp.transpose(jnp.broadcast_to(column, (n, 128)))[0:1, :]


def kernel(
    shape,
    heads_hbm,
    new_ref,
    vec_hbm,
    ids_hbm,
    density_ref,
    spread_ref,
    reassign_ref,
    heads,
    vec_ref,
    ids_ref,
    half_sq,
    table,
    ids_all,
    row_out,
    row_in,
    part_out,
    part_in,
    sum_out,
    sum_in,
    heads_sem,
    own_sem,
    ring_send,
    ring_recv,
    side_send,
    side_recv,
    twin_send,
    twin_recv,
    line_send,
    line_recv,
    ids_send,
    ids_recv,
    know_x,
    know_z,
    row_send,
    row_recv,
    part_send,
    part_recv,
    sum_send,
    sum_recv,
):
    groups, members, depth, total_heads = shape
    chips = groups // 2
    across = members // depth
    here = lax.axis_index("group")
    me = lax.axis_index("member")
    y = here // 2
    core = here % 2
    x = me // depth
    z = me % depth
    twin = y * 2 + (1 - core)
    head_dev, width = heads.shape
    block = new_ref.shape[0]
    near = ids_ref.shape[1]
    posts = vec_ref.shape[0]
    pair = 2 * block
    scale = width / 2.0
    shade = lax.rem(x + 2 * z, SHADES)
    piece = block // SHADES

    def chip(step):
        return lax.rem(y + step + chips, chips)

    def beside_x(step):
        return (here, lax.rem(x + step + across, across) * depth + z)

    def beside_z(step):
        return (here, x * depth + lax.rem(z + step + depth, depth))

    def signal(sem, device):
        pl.semaphore_signal(sem, inc=1, device_id=device, device_id_type=pl.DeviceIdType.MESH)

    def remote(src, dst, send, recv, device):
        return pltpu.make_async_remote_copy(
            src_ref=src,
            dst_ref=dst,
            send_sem=send,
            recv_sem=recv,
            device_id=device,
            device_id_type=pl.DeviceIdType.MESH,
        )

    barrier = pltpu.get_barrier_semaphore()
    for device in (
        (chip(1) * 2 + core, me),
        (chip(-1) * 2 + core, me),
        (chip(2) * 2 + core, me),
        (chip(-2) * 2 + core, me),
        (twin, me),
        beside_z(1),
        beside_z(-1),
        beside_x(1),
        beside_x(-1),
    ):
        signal(barrier, device)

    heads_copy = pltpu.make_async_copy(heads_hbm, heads, heads_sem)
    own = pltpu.make_async_copy(
        new_ref, table.at[pl.ds(pl.multiple_of(core * block, block), block)], own_sem.at[0]
    )
    own_vec = pltpu.make_async_copy(vec_hbm, vec_ref, own_sem.at[1])
    own_ids = pltpu.make_async_copy(ids_hbm, ids_ref, own_sem.at[2])
    own_ids.start()
    own.start()
    heads_copy.start()
    own_vec.start()

    def rows_at(slot, which, first, count):
        start = pl.multiple_of(slot * pair + which * block + first, 16)
        return table.at[pl.ds(start, count)]

    def hop(src, slot, step):
        remote(
            src,
            rows_at(slot, core, shade * piece, piece),
            ring_send,
            ring_recv.at[slot],
            (chip(step) * 2 + core, me),
        ).start()

    def first_hop(slot):
        hop(new_ref.at[pl.ds(pl.multiple_of(shade * piece, 16), piece)], slot, -SLOTS[slot])

    def next_hop(slot, after, step):
        hop(rows_at(slot, core, shade * piece, piece), after, step)

    def arrive(slot):
        mine = rows_at(slot, core, shade * piece, piece)
        pltpu.make_async_copy(mine, mine, ring_recv.at[slot]).wait()

    def spread_out(slot):
        mine = rows_at(slot, core, shade * piece, piece)
        if slot == ACROSS:
            way = 1 - 2 * core
        else:
            way = -1 if SLOTS[slot] > 0 else 1
        for device in (beside_x(1), beside_x(-1), beside_z(way)):
            remote(mine, mine, side_send, side_recv.at[slot], device).start()

    def give_twin(slot):
        others = rows_at(slot, core, 0, block - piece)
        pltpu.make_async_copy(others, others, side_recv.at[slot]).wait()
        whole = rows_at(slot, core, 0, block)
        remote(whole, whole, twin_send, twin_recv.at[slot], (twin, me)).start()

    def twin_wait(slot):
        there = rows_at(slot, 1 - core, 0, block)
        pltpu.make_async_copy(there, there, twin_recv.at[slot]).wait()

    pl.semaphore_wait(barrier, 9)

    for slot in (1, 2, 3, 4):
        first_hop(slot)
    signal(know_x, beside_x(-1))
    for way in (1, -1):
        signal(know_z.at[0], beside_z(way))

    line_own = pltpu.make_async_copy(ids_hbm, ids_all.at[z, x], line_recv)
    line_own.start()

    def send_line(step):
        remote(ids_hbm, ids_all.at[z, x], line_send, line_recv, beside_x(step)).start()

    send_line(1)
    send_line(-1)
    remote(new_ref, rows_at(0, core, 0, block), twin_send, twin_recv.at[0], (twin, me)).start()
    pl.semaphore_wait(know_x, 1)
    for step in range(2, across - 1):
        send_line(step)
    pl.semaphore_wait(know_z.at[0], 2)
    for way in (1, -1):
        signal(know_z.at[1], beside_z(way))

    def square_heads():
        heads_copy.wait()

        def square(t, c):
            at = pl.ds(pl.multiple_of(t * tile, tile), tile)
            h = heads[at, :].astype(F32)
            half_sq[at, :] = jnp.broadcast_to(
                0.5 * jnp.sum(h * h, axis=1, keepdims=True), (tile, 128)
            )
            return c

        lax.fori_loop(0, head_dev // tile, square, 0)

    def know_all():
        pl.semaphore_wait(know_z.at[1], 2)
        for way in (1, -1):
            signal(know_z.at[2], beside_z(way))

    def send_lists():
        pltpu.make_async_copy(ids_all.at[z], ids_all.at[z], line_recv).wait()
        pl.semaphore_wait(know_z.at[2], 2)

        def send(j, c):
            remote(ids_all.at[z], ids_all.at[z], ids_send, ids_recv, beside_z(j)).start()
            return c

        lax.fori_loop(1, depth, send, 0)

    tile = 256

    def crowding(start, count):
        blk = table[pl.ds(start, count), :]
        b32 = blk.astype(F32)
        query = row_of(0.5 * jnp.sum(b32 * b32, axis=1, keepdims=True))
        acc_w = jnp.zeros((8, count), F32)
        acc_we = jnp.zeros((8, count), F32)
        for t in range(0, head_dev, 512):
            dots = lax.dot_general(
                heads[t : t + 512, :], blk, NT, preferred_element_type=F32
            )
            hs = jnp.concatenate([half_sq[t : t + 512, :]] * (count // 128), axis=1)
            u = (hs + query) - dots
            r = 1.0 / (u + scale)
            w = r * r
            we = w * u
            acc_w += jnp.sum(w.reshape(512 // 8, 8, count), axis=0)
            acc_we += jnp.sum(we.reshape(512 // 8, 8, count), axis=0)
        w = (scale * scale) * jnp.sum(acc_w, axis=0, keepdims=True)
        we = scale * jnp.sum(acc_we, axis=0, keepdims=True)
        return w, we

    def send_parts(slot, w, we):
        part_out[slot] = jnp.concatenate([w, we], axis=1)
        if slot == 0:
            pltpu.make_async_copy(part_out.at[slot], part_in.at[here], part_recv).start()
            remote(part_out.at[slot], part_in.at[here], part_send, part_recv, (twin, me)).start()
        else:
            for c in range(2):
                remote(
                    part_out.at[slot],
                    part_in.at[here],
                    part_send,
                    part_recv,
                    (chip(SLOTS[slot]) * 2 + c, me),
                ).start()

    def unit(first, count):
        w, we = crowding(first * pair, count * pair)
        for i in range(count):
            lanes = slice(i * pair, (i + 1) * pair)
            send_parts(first + i, w[:, lanes], we[:, lanes])

    def pick_rows():
        others = ids_all.at[pl.ds(0, depth - 1)]
        pltpu.make_async_copy(others, others, ids_recv).wait()
        ids = ids_all[...].reshape(members, near)
        owner = ids // head_dev
        local = (ids - owner * head_dev).astype(F32)
        held = owner == me
        before = (
            lax.broadcasted_iota(jnp.int32, (near, near), 0)
            < lax.broadcasted_iota(jnp.int32, (near, near), 1)
        ).astype(F32)
        rank = jnp.dot(
            held.astype(F32).astype(BF16), before.astype(BF16), preferred_element_type=F32
        )
        columns = []
        for r in range(MOST):
            hit = jnp.where(held & (rank == float(r)), local + 1.0, 0.0)
            columns.append(jnp.sum(hit, axis=1, keepdims=True) - 1.0)
        column = jnp.concatenate(columns, axis=0)
        slots = MOST * members
        picked = jnp.zeros((slots, width), F32)
        for t in range(head_dev // tile):
            lane = (lax.broadcasted_iota(jnp.int32, (slots, tile), 1) + t * tile).astype(F32)
            onehot = (lane == column).astype(F32).astype(BF16)
            picked += jnp.dot(
                onehot, heads[t * tile : (t + 1) * tile, :], preferred_element_type=F32
            )
        picked = picked.astype(BF16)
        cut = row_out.shape[2]
        place = lax.broadcasted_iota(jnp.int32, (members * 16, slots), 0)
        slot = lax.broadcasted_iota(jnp.int32, (members * 16, slots), 1)
        target = lax.rem(slot, members) * 16 + slot // members
        packed = jnp.zeros((members * 16, cut), F32)
        for c in range(width // cut):
            move = (place == target + MOST * c).astype(F32).astype(BF16)
            packed += jnp.dot(
                move, picked[:, c * cut : (c + 1) * cut], preferred_element_type=F32
            )
        row_out[...] = packed.astype(BF16).reshape(members, 16, cut)
        pltpu.make_async_copy(row_out.at[z * across + x], row_in.at[me], row_recv).start()

        def send(j, c):
            to = lax.rem(me + j, members)
            at = lax.rem(to, depth) * across + to // depth
            remote(row_out.at[at], row_in.at[me], row_send, row_recv, (here, to)).start()
            return c

        lax.fori_loop(1, members, send, 0)

    def finish_rows():
        own_ids.wait()
        own_vec.wait()
        pltpu.make_async_copy(row_in, row_in, row_recv).wait()
        cut = row_in.shape[2]
        owner = jnp.broadcast_to((ids_ref[...] // head_dev).astype(F32), (near, near))
        i = lax.broadcasted_iota(jnp.int32, (near, near), 0)
        j = lax.broadcasted_iota(jnp.int32, (near, near), 1)
        column = jnp.sum(jnp.where(i == j, owner, 0.0), axis=1, keepdims=True)
        rank = jnp.sum(
            jnp.where((owner == column) & (j < i), 1.0, 0.0), axis=1, keepdims=True
        )
        got = row_in[...].reshape(members * 16, cut)
        lane = lax.broadcasted_iota(jnp.int32, (near, members * 16), 1).astype(F32)
        want = column * 16.0 + rank
        dots = jnp.zeros((near, posts), F32)
        row_sq = jnp.zeros((near, 1), F32)
        vec_sq = jnp.zeros((posts, 1), F32)
        for c in range(width // cut):
            choose = (lane == want + float(MOST * c)).astype(F32).astype(BF16)
            rows = jnp.dot(choose, got, preferred_element_type=F32)
            vec = vec_ref[:, c * cut : (c + 1) * cut]
            v32 = vec.astype(F32)
            row_sq += jnp.sum(rows * rows, axis=1, keepdims=True)
            vec_sq += jnp.sum(v32 * v32, axis=1, keepdims=True)
            dots += lax.dot_general(rows.astype(BF16), vec, NT, preferred_element_type=F32)
        reassign_ref[...] = (row_sq + row_of(vec_sq) - 2.0 * dots) / width

    square_heads()
    for slot, after, step in ((1, 5, 2), (2, 6, -2)):
        arrive(slot)
        spread_out(slot)
        next_hop(slot, after, step)
    know_all()
    for slot in (3, 4):
        arrive(slot)
        spread_out(slot)
    next_hop(3 + core, ACROSS, 2 - 4 * core)
    send_lists()
    for slot in (1, 2, 3, 4):
        give_twin(slot)
    for slot in (5, 6, ACROSS):
        arrive(slot)
        spread_out(slot)
    own.wait()
    for slot in range(4):
        twin_wait(slot)
    unit(0, 4)
    for slot in (5, 6, ACROSS):
        give_twin(slot)
    pick_rows()
    for slot in range(4, 8):
        twin_wait(slot)
    unit(4, 4)

    pltpu.make_async_copy(part_in, part_in, part_recv).wait()
    sum_out[...] = jnp.sum(part_in[...], axis=0)
    pltpu.make_async_copy(sum_out, sum_in.at[me], sum_recv).start()

    def send_sum(j, c):
        remote(sum_out, sum_in.at[me], sum_send, sum_recv, (here, lax.rem(me + j, members))).start()
        return c

    lax.fori_loop(1, members, send_sum, 0)
    finish_rows()
    pltpu.make_async_copy(sum_in, sum_in, sum_recv).wait()
    total = jnp.sum(sum_in[...], axis=0)
    w = total[:, 0:pair]
    we = total[:, pair : 2 * pair]
    w = jnp.where(core == 0, w[:, 0:block], w[:, block:pair])
    we = jnp.where(core == 0, we[:, 0:block], we[:, block:pair])
    density_ref[...] = jnp.log(w / float(total_heads))
    spread_ref[...] = we / w

    for sem, count in ((ring_send, 7 * piece), (side_send, 21 * piece), (twin_send, 8 * block)):
        sent = table.at[pl.ds(0, count)]
        pltpu.make_async_copy(sent, sent, sem).wait()
    others = pl.ds(0, members - 1)
    lines = ids_all.at[0, pl.ds(0, across - 1)]
    pltpu.make_async_copy(lines, lines, line_send).wait()
    lists = ids_all.at[pl.ds(0, depth - 1)]
    pltpu.make_async_copy(lists, lists, ids_send).wait()
    pltpu.make_async_copy(row_in.at[others], row_in.at[others], row_send).wait()
    pltpu.make_async_copy(sum_in.at[others], sum_in.at[others], sum_send).wait()
    others = pl.ds(0, groups - 1)
    pltpu.make_async_copy(part_in.at[others], part_in.at[others], part_send).wait()


def per_device(heads, new_heads, vectors, near_ids):
    groups = lax.axis_size("group")
    members = lax.axis_size("member")
    head_dev, width = heads.shape
    block = new_heads.shape[0]
    posts = vectors.shape[1]
    near = near_ids.shape[1]
    depth = 8
    anywhere = pl.BlockSpec(memory_space=pltpu.HBM)
    vmem = pl.BlockSpec(memory_space=pltpu.VMEM)
    dma = pltpu.SemaphoreType.DMA
    density, spread, reassign = pl.pallas_call(
        functools.partial(kernel, (groups, members, depth, head_dev * groups * members)),
        out_shape=(
            jax.ShapeDtypeStruct((1, block), F32),
            jax.ShapeDtypeStruct((1, block), F32),
            jax.ShapeDtypeStruct((near, posts), F32),
        ),
        in_specs=[anywhere] * 4,
        out_specs=(vmem, vmem, vmem),
        scratch_shapes=[
            pltpu.VMEM((head_dev, width), BF16),
            pltpu.VMEM((posts, width), BF16),
            pltpu.VMEM((1, near), jnp.int32),
            pltpu.VMEM((head_dev, 128), F32),
            pltpu.VMEM((groups * block, width), BF16),
            pltpu.VMEM((depth, members // depth, 1, near), jnp.int32),
            pltpu.VMEM((members, 16, 256), BF16),
            pltpu.VMEM((members, 16, 256), BF16),
            pltpu.VMEM((groups // 2, 1, 4 * block), F32),
            pltpu.VMEM((groups, 1, 4 * block), F32),
            pltpu.VMEM((1, 4 * block), F32),
            pltpu.VMEM((members, 1, 4 * block), F32),
            dma,
            dma((3,)),
            dma,
            dma((8,)),
            dma,
            dma((8,)),
            dma,
            dma((8,)),
            dma,
            dma,
            dma,
            dma,
            pltpu.SemaphoreType.REGULAR,
            pltpu.SemaphoreType.REGULAR((3,)),
            dma,
            dma,
            dma,
            dma,
            dma,
            dma,
        ],
        compiler_params=pltpu.CompilerParams(
            collective_id=0, has_side_effects=True, vmem_limit_bytes=60 * 1024 * 1024
        ),
    )(heads, new_heads, vectors[0], near_ids)
    return density[0], spread[0], reassign[None]


def solution(mesh):
    placed = (
        P(("group", "member"), None),
        P("group", None),
        P(("group", "member"), None, None),
        P(("group", "member"), None),
    )
    return jax.shard_map(
        per_device,
        mesh=mesh,
        in_specs=placed,
        out_specs=(P("group"), P("group"), P(("group", "member"), None, None)),
        check_vma=False,
    )
```

time: 54.8 us -> 46.3 us (0.84)
  Pallas kernels: 47.9 us -> 41.8 us
  local copies, waits for them, and re-layouts: 5.99 us -> 3.7 us
    pallas_call x1, Pallas kernels: 47.9 us -> 41.8 us  [per_device(): pl.pallas_call(functools.partial(kernel, (groups, members, depth, head_de...]
    unnamed x11 -> x3, local copies, waits for them, and re-layouts: 5.99 us -> 3.7 us
where the time goes in v2:
time: 46.3 us; the launch traced here: 46.1 us
  Pallas kernels  41.8 us (90%)
  local copies, waits for them, and re-layouts  3.7 us (8%)
  between operations  0.64 us (1%)
    pallas_call x1, Pallas kernels, per_device(): pl.pallas_call(functools.partial(kernel, (groups, members, depth, head_de...  41.8 us
    unnamed x3, local copies, waits for them, and re-layouts  3.7 us

profile of v2, /device:TPU:1, one launch (start us, length us, event | category | flops | bytes accessed | tf_op | source)
XLA Modules:
  0.0 46.1 jit_solution(11439538931389397588)
XLA Ops:
  0.6 41.8 %shard_map.67 = (f32[1,64]{1,0:T(1,128)}, f32[1,64]{1,0:T(1,128)}, f32[64,128]{1,0:T(8,128)}) custom-call(bf16[2048,768]{1,0:T(8,128)(2,1)} %heads_hbm.1, bf16[64,768]{1,0:T(8,128)(2,1)} %new_ref.1, bf16[128,768]{1,0:T(8,128)(2,1)} %bitcast.4, s32[1,64]{1,0:T(1,128)} %ids_hbm.1), custom_call_target="tpu_custom_call" | custom-call | tf_op jit(solution)/shard_map/pallas_call | solution.py:418
  42.4 1.2 %copy.10 = f32[64]{0:T(128)} copy(f32[64]{0:T(128)} %bitcast.7) | data formatting | bytes 512
  43.6 1.1 %copy.11 = f32[64]{0:T(128)} copy(f32[64]{0:T(128)} %bitcast.6) | data formatting | bytes 512
  44.8 1.4 %copy.12 = f32[1,64,128]{2,1,0:T(8,128)} copy(f32[1,64,128]{2,1,0:T(8,128)} %bitcast.5) | data formatting | bytes 65536

commit v3 on v2

v3 whole, which is shorter than its diff:
```python
import functools

import jax
import jax.numpy as jnp
from jax import lax
from jax.experimental import pallas as pl
from jax.experimental.pallas import tpu as pltpu
from jax.sharding import PartitionSpec as P

F32 = jnp.float32
BF16 = jnp.bfloat16
MOST = 4
SHADES = 4
SLOTS = (0, -1, 1, -2, 2, -3, 3, 4)
ACROSS = 7
NT = (((1,), (1,)), ((), ()))


def row_of(column):
    n = column.shape[0]
    return jnp.transpose(jnp.broadcast_to(column, (n, 128)))[0:1, :]


def kernel(
    shape,
    heads_hbm,
    new_ref,
    vec_hbm,
    ids_hbm,
    result_ref,
    heads,
    vec_ref,
    ids_ref,
    half_sq,
    table,
    ids_all,
    row_out,
    row_in,
    part_out,
    part_in,
    sum_out,
    sum_in,
    heads_sem,
    own_sem,
    ring_send,
    ring_recv,
    side_send,
    side_recv,
    twin_send,
    twin_recv,
    line_send,
    line_recv,
    ids_send,
    ids_recv,
    know_x,
    know_z,
    row_send,
    row_recv,
    part_send,
    part_recv,
    sum_send,
    sum_recv,
):
    groups, members, depth, total_heads = shape
    chips = groups // 2
    across = members // depth
    here = lax.axis_index("group")
    me = lax.axis_index("member")
    y = here // 2
    core = here % 2
    x = me // depth
    z = me % depth
    twin = y * 2 + (1 - core)
    head_dev, width = heads_hbm.shape
    block = new_ref.shape[0]
    near = ids_ref.shape[1]
    posts = vec_ref.shape[0]
    scale = width / 2.0
    far_first = sorted(
        [(i, j) for i in range(across) for j in range(depth) if i or j],
        key=lambda d: -min(d[0], across - d[0]) - min(d[1], depth - d[1]),
    )
    shade = lax.rem(x + 2 * z, SHADES)
    piece = block // SHADES

    def chip(step):
        return lax.rem(y + step + chips, chips)

    def beside_x(step):
        return (here, lax.rem(x + step + across, across) * depth + z)

    def beside_z(step):
        return (here, x * depth + lax.rem(z + step + depth, depth))

    def signal(sem, device):
        pl.semaphore_signal(sem, inc=1, device_id=device, device_id_type=pl.DeviceIdType.MESH)

    def remote(src, dst, send, recv, device):
        return pltpu.make_async_remote_copy(
            src_ref=src,
            dst_ref=dst,
            send_sem=send,
            recv_sem=recv,
            device_id=device,
            device_id_type=pl.DeviceIdType.MESH,
        )

    barrier = pltpu.get_barrier_semaphore()
    for device in (
        (chip(1) * 2 + core, me),
        (chip(-1) * 2 + core, me),
        (chip(2) * 2 + core, me),
        (chip(-2) * 2 + core, me),
        (twin, me),
        beside_z(1),
        beside_z(-1),
        beside_x(1),
        beside_x(-1),
    ):
        signal(barrier, device)

    held = pl.multiple_of(core * head_dev, head_dev)
    twin_held = pl.multiple_of((1 - core) * head_dev, head_dev)
    heads_copy = pltpu.make_async_copy(heads_hbm, heads.at[pl.ds(held, head_dev)], heads_sem)
    own = pltpu.make_async_copy(new_ref, table.at[pl.ds(0, block)], own_sem.at[0])
    own_vec = pltpu.make_async_copy(vec_hbm, vec_ref, own_sem.at[1])
    own_ids = pltpu.make_async_copy(ids_hbm, ids_ref, own_sem.at[2])
    own_ids.start()
    own.start()
    heads_copy.start()
    own_vec.start()

    def rows_at(slot, first, count):
        return table.at[pl.ds(pl.multiple_of(slot * block + first, 16), count)]

    def hop(src, slot, step):
        remote(
            src,
            rows_at(slot, shade * piece, piece),
            ring_send,
            ring_recv.at[slot],
            (chip(step) * 2 + core, me),
        ).start()

    def first_hop(slot):
        hop(new_ref.at[pl.ds(pl.multiple_of(shade * piece, 16), piece)], slot, -SLOTS[slot])

    def next_hop(slot, after, step):
        hop(rows_at(slot, shade * piece, piece), after, step)

    def arrive(slot):
        mine = rows_at(slot, shade * piece, piece)
        pltpu.make_async_copy(mine, mine, ring_recv.at[slot]).wait()

    def spread_out(slot):
        mine = rows_at(slot, shade * piece, piece)
        if slot == ACROSS:
            way = 1 - 2 * core
        else:
            way = -1 if SLOTS[slot] > 0 else 1
        for device in (beside_x(1), beside_x(-1), beside_z(way)):
            remote(mine, mine, side_send, side_recv.at[slot], device).start()

    def whole(slot):
        others = rows_at(slot, 0, block - piece)
        pltpu.make_async_copy(others, others, side_recv.at[slot]).wait()

    pl.semaphore_wait(barrier, 9)

    for slot in (3, 4, 1, 2):
        first_hop(slot)
    signal(know_x, beside_x(-1))
    for way in (1, -1):
        signal(know_z.at[0], beside_z(way))

    line_own = pltpu.make_async_copy(ids_hbm, ids_all.at[z, x], line_recv)
    line_own.start()

    def send_line(step):
        remote(ids_hbm, ids_all.at[z, x], line_send, line_recv, beside_x(step)).start()

    send_line(1)
    send_line(-1)
    twin_heads = remote(
        heads_hbm, heads.at[pl.ds(held, head_dev)], twin_send, twin_recv, (twin, me)
    )
    twin_heads.start()
    pl.semaphore_wait(know_x, 1)
    for step in range(2, across - 1):
        send_line(step)
    pl.semaphore_wait(know_z.at[0], 2)
    for way in (1, -1):
        signal(know_z.at[1], beside_z(way))

    def square_heads(first):
        def square(t, c):
            at = pl.ds(pl.multiple_of(first + t * tile, tile), tile)
            h = heads[at, :].astype(F32)
            half_sq[at, :] = jnp.broadcast_to(
                0.5 * jnp.sum(h * h, axis=1, keepdims=True), (tile, 128)
            )
            return c

        lax.fori_loop(0, head_dev // tile, square, 0)

    def know_all():
        pl.semaphore_wait(know_z.at[1], 2)
        for way in (1, -1):
            signal(know_z.at[2], beside_z(way))

    def send_lists():
        pltpu.make_async_copy(ids_all.at[z], ids_all.at[z], line_recv).wait()
        pl.semaphore_wait(know_z.at[2], 2)

        def send(j, c):
            remote(ids_all.at[z], ids_all.at[z], ids_send, ids_recv, beside_z(j)).start()
            return c

        lax.fori_loop(1, depth, send, 0)

    tile = 256

    def crowding(start, count):
        blk = table[pl.ds(start, count), :]
        b32 = blk.astype(F32)
        query = row_of(0.5 * jnp.sum(b32 * b32, axis=1, keepdims=True))
        acc_w = jnp.zeros((8, count), F32)
        acc_we = jnp.zeros((8, count), F32)
        for t in range(0, 2 * head_dev, tile):
            dots = lax.dot_general(
                heads[t : t + tile, :], blk, NT, preferred_element_type=F32
            )
            hs = jnp.concatenate([half_sq[t : t + tile, :]] * (count // 128), axis=1)
            u = (hs + query) - dots
            r = 1.0 / (u + scale)
            w = r * r
            we = w * u
            acc_w += jnp.sum(w.reshape(tile // 8, 8, count), axis=0)
            acc_we += jnp.sum(we.reshape(tile // 8, 8, count), axis=0)
        w = (scale * scale) * jnp.sum(acc_w, axis=0, keepdims=True)
        we = scale * jnp.sum(acc_we, axis=0, keepdims=True)
        return w, we

    def send_parts(slot, w, we):
        part_out[slot] = jnp.concatenate([w, we], axis=1)
        if slot == 0:
            pltpu.make_async_copy(part_out.at[slot], part_in.at[y], part_recv).start()
        else:
            remote(
                part_out.at[slot],
                part_in.at[y],
                part_send,
                part_recv,
                (chip(SLOTS[slot]) * 2 + core, me),
            ).start()

    def unit(first, count):
        w, we = crowding(first * block, count * block)
        for i in reversed(range(count)):
            lanes = slice(i * block, (i + 1) * block)
            send_parts(first + i, w[:, lanes], we[:, lanes])

    def pick_rows():
        others = ids_all.at[pl.ds(0, depth - 1)]
        pltpu.make_async_copy(others, others, ids_recv).wait()
        ids = ids_all[...].reshape(members, near)
        owner = ids // head_dev
        local = (ids - owner * head_dev).astype(F32)
        listed = owner == me
        before = (
            lax.broadcasted_iota(jnp.int32, (near, near), 0)
            < lax.broadcasted_iota(jnp.int32, (near, near), 1)
        ).astype(F32)
        rank = jnp.dot(
            listed.astype(F32).astype(BF16), before.astype(BF16), preferred_element_type=F32
        )
        columns = []
        for r in range(MOST):
            hit = jnp.where(listed & (rank == float(r)), local + 1.0, 0.0)
            columns.append(jnp.sum(hit, axis=1, keepdims=True) - 1.0)
        column = jnp.concatenate(columns, axis=0)
        slots = MOST * members
        picked = jnp.zeros((slots, width), F32)
        for t in range(head_dev // tile):
            at = pl.ds(pl.multiple_of(held + t * tile, tile), tile)
            lane = (lax.broadcasted_iota(jnp.int32, (slots, tile), 1) + t * tile).astype(F32)
            onehot = (lane == column).astype(F32).astype(BF16)
            picked += jnp.dot(onehot, heads[at, :], preferred_element_type=F32)
        picked = picked.astype(BF16)
        cut = row_out.shape[2]
        place = lax.broadcasted_iota(jnp.int32, (members * 16, slots), 0)
        slot = lax.broadcasted_iota(jnp.int32, (members * 16, slots), 1)
        target = lax.rem(slot, members) * 16 + slot // members
        packed = jnp.zeros((members * 16, cut), F32)
        for c in range(width // cut):
            move = (place == target + MOST * c).astype(F32).astype(BF16)
            packed += jnp.dot(
                move, picked[:, c * cut : (c + 1) * cut], preferred_element_type=F32
            )
        row_out[...] = packed.astype(BF16).reshape(members, 16, cut)
        pltpu.make_async_copy(row_out.at[z * across + x], row_in.at[me], row_recv).start()

        for dx, dz in far_first:
            to_x = lax.rem(x + dx, across)
            to_z = lax.rem(z + dz, depth)
            remote(
                row_out.at[to_z * across + to_x],
                row_in.at[me],
                row_send,
                row_recv,
                (here, to_x * depth + to_z),
            ).start()

    def finish_rows():
        own_ids.wait()
        own_vec.wait()
        pltpu.make_async_copy(row_in, row_in, row_recv).wait()
        cut = row_in.shape[2]
        owner = jnp.broadcast_to((ids_ref[...] // head_dev).astype(F32), (near, near))
        i = lax.broadcasted_iota(jnp.int32, (near, near), 0)
        j = lax.broadcasted_iota(jnp.int32, (near, near), 1)
        column = jnp.sum(jnp.where(i == j, owner, 0.0), axis=1, keepdims=True)
        rank = jnp.sum(
            jnp.where((owner == column) & (j < i), 1.0, 0.0), axis=1, keepdims=True
        )
        got = row_in[...].reshape(members * 16, cut)
        lane = lax.broadcasted_iota(jnp.int32, (near, members * 16), 1).astype(F32)
        want = column * 16.0 + rank
        dots = jnp.zeros((near, posts), F32)
        row_sq = jnp.zeros((near, 1), F32)
        vec_sq = jnp.zeros((posts, 1), F32)
        for c in range(width // cut):
            choose = (lane == want + float(MOST * c)).astype(F32).astype(BF16)
            rows = jnp.dot(choose, got, preferred_element_type=F32)
            vec = vec_ref[:, c * cut : (c + 1) * cut]
            v32 = vec.astype(F32)
            row_sq += jnp.sum(rows * rows, axis=1, keepdims=True)
            vec_sq += jnp.sum(v32 * v32, axis=1, keepdims=True)
            dots += lax.dot_general(rows.astype(BF16), vec, NT, preferred_element_type=F32)
        result_ref[0:near, :] = (row_sq + row_of(vec_sq) - 2.0 * dots) / width

    heads_copy.wait()
    square_heads(held)
    for slot, after, step in ((1, 5, 2), (2, 6, -2)):
        arrive(slot)
        spread_out(slot)
        next_hop(slot, after, step)
    know_all()
    for slot in (3, 4):
        arrive(slot)
        spread_out(slot)
    next_hop(3 + core, ACROSS, 2 - 4 * core)
    send_lists()
    for slot in (5, 6, ACROSS):
        arrive(slot)
        spread_out(slot)
    twin_heads.wait_recv()
    square_heads(twin_held)
    own.wait()
    for slot in (1, 2, 3):
        whole(slot)
    unit(0, 4)
    for slot in (4, 5, 6, ACROSS):
        whole(slot)
    unit(4, 4)
    pick_rows()

    pltpu.make_async_copy(part_in, part_in, part_recv).wait()
    sum_out[...] = jnp.sum(part_in[...], axis=0)
    pltpu.make_async_copy(sum_out, sum_in.at[me], sum_recv).start()

    for dx, dz in far_first:
        to = lax.rem(x + dx, across) * depth + lax.rem(z + dz, depth)
        remote(sum_out, sum_in.at[me], sum_send, sum_recv, (here, to)).start()
    finish_rows()
    pltpu.make_async_copy(sum_in, sum_in, sum_recv).wait()
    total = jnp.sum(sum_in[...], axis=0)
    w = total[:, 0:block]
    we = total[:, block : 2 * block]
    result_ref[near : near + 1, 0:block] = jnp.log(w / float(total_heads))
    result_ref[near : near + 1, 64 : 64 + block] = we / w

    for sem, count in ((ring_send, 7 * piece), (side_send, 21 * piece)):
        sent = table.at[pl.ds(0, count)]
        pltpu.make_async_copy(sent, sent, sem).wait()
    twin_heads.wait_send()
    others = pl.ds(0, members - 1)
    lines = ids_all.at[0, pl.ds(0, across - 1)]
    pltpu.make_async_copy(lines, lines, line_send).wait()
    lists = ids_all.at[pl.ds(0, depth - 1)]
    pltpu.make_async_copy(lists, lists, ids_send).wait()
    pltpu.make_async_copy(row_in.at[others], row_in.at[others], row_send).wait()
    pltpu.make_async_copy(sum_in.at[others], sum_in.at[others], sum_send).wait()
    others = pl.ds(0, chips - 1)
    pltpu.make_async_copy(part_in.at[others], part_in.at[others], part_send).wait()


def part(result_ref, density_ref, spread_ref, reassign_ref):
    near, block = reassign_ref.shape[0], density_ref.shape[1]
    density_ref[...] = result_ref[near : near + 1, 0:block]
    spread_ref[...] = result_ref[near : near + 1, 64 : 64 + block]
    reassign_ref[...] = result_ref[0:near, :]


def per_device(heads, new_heads, vectors, near_ids):
    groups = lax.axis_size("group")
    members = lax.axis_size("member")
    head_dev, width = heads.shape
    block = new_heads.shape[0]
    posts = vectors.shape[1]
    near = near_ids.shape[1]
    depth = 8
    anywhere = pl.BlockSpec(memory_space=pltpu.HBM)
    vmem = pl.BlockSpec(memory_space=pltpu.VMEM)
    dma = pltpu.SemaphoreType.DMA
    result = pl.pallas_call(
        functools.partial(kernel, (groups, members, depth, head_dev * groups * members)),
        out_shape=jax.ShapeDtypeStruct((near + 8, posts), F32),
        in_specs=[anywhere] * 4,
        out_specs=vmem,
        scratch_shapes=[
            pltpu.VMEM((2 * head_dev, width), BF16),
            pltpu.VMEM((posts, width), BF16),
            pltpu.VMEM((1, near), jnp.int32),
            pltpu.VMEM((2 * head_dev, 128), F32),
            pltpu.VMEM((groups // 2 * block, width), BF16),
            pltpu.VMEM((depth, members // depth, 1, near), jnp.int32),
            pltpu.VMEM((members, 16, 256), BF16),
            pltpu.VMEM((members, 16, 256), BF16),
            pltpu.VMEM((groups // 2, 1, 2 * block), F32),
            pltpu.VMEM((groups // 2, 1, 2 * block), F32),
            pltpu.VMEM((1, 2 * block), F32),
            pltpu.VMEM((members, 1, 2 * block), F32),
            dma,
            dma((3,)),
            dma,
            dma((8,)),
            dma,
            dma((8,)),
            dma,
            dma,
            dma,
            dma,
            dma,
            dma,
            pltpu.SemaphoreType.REGULAR,
            pltpu.SemaphoreType.REGULAR((3,)),
            dma,
            dma,
            dma,
            dma,
            dma,
            dma,
        ],
        compiler_params=pltpu.CompilerParams(
            collective_id=0, has_side_effects=True, vmem_limit_bytes=60 * 1024 * 1024
        ),
    )(heads, new_heads, vectors[0], near_ids)
    density, spread, reassign = pl.pallas_call(
        part,
        out_shape=(
            jax.ShapeDtypeStruct((1, block), F32),
            jax.ShapeDtypeStruct((1, block), F32),
            jax.ShapeDtypeStruct((near, posts), F32),
        ),
        in_specs=[vmem],
        out_specs=(vmem, vmem, vmem),
    )(result)
    return density[0], spread[0], reassign[None]


def solution(mesh):
    placed = (
        P(("group", "member"), None),
        P("group", None),
        P(("group", "member"), None, None),
        P(("group", "member"), None),
    )
    return jax.shard_map(
        per_device,
        mesh=mesh,
        in_specs=placed,
        out_specs=(P("group"), P("group"), P(("group", "member"), None, None)),
        check_vma=False,
    )
```

time: 46.3 us -> 39.1 us (0.84)
  the two profiles are of different devices: /device:TPU:1 before, /device:TPU:8 now
where the time goes in v3:
time: 39.1 us; the launch traced here: 38.9 us
  Pallas kernels  38.3 us (98%)
  between operations  0.64 us (2%)
    pallas_call x1, Pallas kernels, per_device(): pl.pallas_call(functools.partial(kernel, (groups, members, depth, head_de...  36.9 us
    pallas_call x1, Pallas kernels, per_device(): pl.pallas_call(part, out_shape=(jax.ShapeDtypeStruct((1, block), F32), ja...  1.46 us

profile of v3, /device:TPU:8, one launch (start us, length us, event | category | flops | bytes accessed | tf_op | source)
XLA Modules:
  0.0 38.9 jit_solution(11527279549012451410)
XLA Ops:
  0.6 36.9 %shard_map.67.result_ref = f32[72,128]{1,0:T(8,128)} custom-call(bf16[2048,768]{1,0:T(8,128)(2,1)} %heads_hbm.1, bf16[64,768]{1,0:T(8,128)(2,1)} %new_ref.1, bf16[128,768]{1,0:T(8,128)(2,1)} %bitcast.4, s32[1,64]{1,0:T(1,128)} %ids_hbm.1), custom_call_target="tpu_custom_call" | custom-call | tf_op jit(solution)/shard_map/pallas_call | solution.py:416
  37.5 1.5 %shard_map.68 = (f32[1,64]{1,0:T(1,128)}, f32[1,64]{1,0:T(1,128)}, f32[64,128]{1,0:T(8,128)}) custom-call(f32[72,128]{1,0:T(8,128)} %shard_map.67.result_ref), custom_call_target="tpu_custom_call" | custom-call | tf_op jit(solution)/shard_map/pallas_call | solution.py:459

commit v4 on v3

--- a/solution.py
+++ b/solution.py
@@ -143,7 +143,7 @@
         ).start()
 
     def first_hop(slot):
-        hop(new_ref.at[pl.ds(pl.multiple_of(shade * piece, 16), piece)], slot, -SLOTS[slot])
+        hop(rows_at(0, shade * piece, piece), slot, -SLOTS[slot])
 
     def next_hop(slot, after, step):
         hop(rows_at(slot, shade * piece, piece), after, step)
@@ -165,6 +165,7 @@
         others = rows_at(slot, 0, block - piece)
         pltpu.make_async_copy(others, others, side_recv.at[slot]).wait()
 
+    own.wait()
     pl.semaphore_wait(barrier, 9)
 
     for slot in (3, 4, 1, 2):
@@ -314,7 +315,6 @@
     def finish_rows():
         own_ids.wait()
         own_vec.wait()
-        pltpu.make_async_copy(row_in, row_in, row_recv).wait()
         cut = row_in.shape[2]
         owner = jnp.broadcast_to((ids_ref[...] // head_dev).astype(F32), (near, near))
         i = lax.broadcasted_iota(jnp.int32, (near, near), 0)
@@ -323,40 +323,48 @@
         rank = jnp.sum(
             jnp.where((owner == column) & (j < i), 1.0, 0.0), axis=1, keepdims=True
         )
-        got = row_in[...].reshape(members * 16, cut)
         lane = lax.broadcasted_iota(jnp.int32, (near, members * 16), 1).astype(F32)
         want = column * 16.0 + rank
+        starts = range(0, width, cut)
+        choose = [
+            (lane == want + float(MOST * c)).astype(F32).astype(BF16)
+            for c in range(len(starts))
+        ]
+        v32 = vec_ref[...].astype(F32)
+        vec_sq = row_of(jnp.sum(v32 * v32, axis=1, keepdims=True))
+        pltpu.make_async_copy(row_in, row_in, row_recv).wait()
+        got = row_in[...].reshape(members * 16, cut)
         dots = jnp.zeros((near, posts), F32)
         row_sq = jnp.zeros((near, 1), F32)
-        vec_sq = jnp.zeros((posts, 1), F32)
-        for c in range(width // cut):
-            choose = (lane == want + float(MOST * c)).astype(F32).astype(BF16)
-            rows = jnp.dot(choose, got, preferred_element_type=F32)
-            vec = vec_ref[:, c * cut : (c + 1) * cut]
-            v32 = vec.astype(F32)
+        for c, start in enumerate(starts):
+            rows = jnp.dot(choose[c], got, preferred_element_type=F32)
             row_sq += jnp.sum(rows * rows, axis=1, keepdims=True)
-            vec_sq += jnp.sum(v32 * v32, axis=1, keepdims=True)
-            dots += lax.dot_general(rows.astype(BF16), vec, NT, preferred_element_type=F32)
-        result_ref[0:near, :] = (row_sq + row_of(vec_sq) - 2.0 * dots) / width
+            dots += lax.dot_general(
+                rows.astype(BF16),
+                vec_ref[:, start : start + cut],
+                NT,
+                preferred_element_type=F32,
+            )
+        result_ref[0:near, :] = (row_sq + vec_sq - 2.0 * dots) / width
 
     heads_copy.wait()
     square_heads(held)
-    for slot, after, step in ((1, 5, 2), (2, 6, -2)):
+    for slot in (1, 2):
         arrive(slot)
         spread_out(slot)
+    know_all()
+    for slot, after, step in ((3, 5, 1), (4, 6, -1)):
+        arrive(slot)
         next_hop(slot, after, step)
-    know_all()
+    next_hop(3 + core, ACROSS, 2 - 4 * core)
     for slot in (3, 4):
-        arrive(slot)
         spread_out(slot)
-    next_hop(3 + core, ACROSS, 2 - 4 * core)
-    send_lists()
     for slot in (5, 6, ACROSS):
         arrive(slot)
         spread_out(slot)
+    send_lists()
     twin_heads.wait_recv()
     square_heads(twin_held)
-    own.wait()
     for slot in (1, 2, 3):
         whole(slot)
     unit(0, 4)

time: 39.1 us -> 39.1 us (level)
  no operation moved by 1% of the time
where the time goes in v4:
time: 39.1 us; the launch traced here: 38.9 us
  Pallas kernels  38.3 us (98%)
  between operations  0.64 us (2%)
    pallas_call x1, Pallas kernels, per_device(): pl.pallas_call(functools.partial(kernel, (groups, members, depth, head_de...  36.8 us
    pallas_call x1, Pallas kernels, per_device(): pl.pallas_call(part, out_shape=(jax.ShapeDtypeStruct((1, block), F32), ja...  1.46 us

profile of v4, /device:TPU:8, one launch (start us, length us, event | category | flops | bytes accessed | tf_op | source)
XLA Modules:
  0.0 38.9 jit_solution(1861549684115159715)
XLA Ops:
  0.6 36.8 %shard_map.67.result_ref = f32[72,128]{1,0:T(8,128)} custom-call(bf16[2048,768]{1,0:T(8,128)(2,1)} %heads_hbm.1, bf16[64,768]{1,0:T(8,128)(2,1)} %new_ref.1, bf16[128,768]{1,0:T(8,128)(2,1)} %bitcast.4, s32[1,64]{1,0:T(1,128)} %ids_hbm.1), custom_call_target="tpu_custom_call" | custom-call | tf_op jit(solution)/shard_map/pallas_call | solution.py:424
  37.4 1.5 %shard_map.68 = (f32[1,64]{1,0:T(1,128)}, f32[1,64]{1,0:T(1,128)}, f32[64,128]{1,0:T(8,128)}) custom-call(f32[72,128]{1,0:T(8,128)} %shard_map.67.result_ref), custom_call_target="tpu_custom_call" | custom-call | tf_op jit(solution)/shard_map/pallas_call | solution.py:467

commit v5 on v4

--- a/solution.py
+++ b/solution.py
@@ -221,17 +221,19 @@
 
     tile = 256
 
-    def crowding(start, count):
+    def crowding(start, count, between):
         blk = table[pl.ds(start, count), :]
         b32 = blk.astype(F32)
         query = row_of(0.5 * jnp.sum(b32 * b32, axis=1, keepdims=True))
         acc_w = jnp.zeros((8, count), F32)
         acc_we = jnp.zeros((8, count), F32)
         for t in range(0, 2 * head_dev, tile):
-            dots = lax.dot_general(
-                heads[t : t + tile, :], blk, NT, preferred_element_type=F32
-            )
-            hs = jnp.concatenate([half_sq[t : t + tile, :]] * (count // 128), axis=1)
+            if t == head_dev:
+                between()
+            first = held if t < head_dev else twin_held
+            at = pl.ds(pl.multiple_of(first + t % head_dev, tile), tile)
+            dots = lax.dot_general(heads[at, :], blk, NT, preferred_element_type=F32)
+            hs = jnp.concatenate([half_sq[at, :]] * (count // 128), axis=1)
             u = (hs + query) - dots
             r = 1.0 / (u + scale)
             w = r * r
@@ -255,8 +257,8 @@
                 (chip(SLOTS[slot]) * 2 + core, me),
             ).start()
 
-    def unit(first, count):
-        w, we = crowding(first * block, count * block)
+    def unit(first, count, between):
+        w, we = crowding(first * block, count * block, between)
         for i in reversed(range(count)):
             lanes = slice(i * block, (i + 1) * block)
             send_parts(first + i, w[:, lanes], we[:, lanes])
@@ -363,14 +365,17 @@
         arrive(slot)
         spread_out(slot)
     send_lists()
-    twin_heads.wait_recv()
-    square_heads(twin_held)
     for slot in (1, 2, 3):
         whole(slot)
-    unit(0, 4)
+
+    def take_twin():
+        twin_heads.wait_recv()
+        square_heads(twin_held)
+
+    unit(0, 4, take_twin)
     for slot in (4, 5, 6, ACROSS):
         whole(slot)
-    unit(4, 4)
+    unit(4, 4, lambda: None)
     pick_rows()
 
     pltpu.make_async_copy(part_in, part_in, part_recv).wait()

time: 39.1 us -> 39.1 us (level)
  no operation moved by 1% of the time
where the time goes in v5:
time: 39.1 us; the launch traced here: 38.9 us
  Pallas kernels  38.3 us (98%)
  between operations  0.64 us (2%)
    pallas_call x1, Pallas kernels, per_device(): pl.pallas_call(functools.partial(kernel, (groups, members, depth, head_de...  36.8 us
    pallas_call x1, Pallas kernels, per_device(): pl.pallas_call(part, out_shape=(jax.ShapeDtypeStruct((1, block), F32), ja...  1.46 us

profile of v5, /device:TPU:8, one launch (start us, length us, event | category | flops | bytes accessed | tf_op | source)
XLA Modules:
  0.0 38.9 jit_solution(8149226070351229765)
XLA Ops:
  0.6 36.8 %shard_map.67.result_ref = f32[72,128]{1,0:T(8,128)} custom-call(bf16[2048,768]{1,0:T(8,128)(2,1)} %heads_hbm.1, bf16[64,768]{1,0:T(8,128)(2,1)} %new_ref.1, bf16[128,768]{1,0:T(8,128)(2,1)} %bitcast.4, s32[1,64]{1,0:T(1,128)} %ids_hbm.1), custom_call_target="tpu_custom_call" | custom-call | tf_op jit(solution)/shard_map/pallas_call | solution.py:429
  37.5 1.5 %shard_map.68 = (f32[1,64]{1,0:T(1,128)}, f32[1,64]{1,0:T(1,128)}, f32[64,128]{1,0:T(8,128)}) custom-call(f32[72,128]{1,0:T(8,128)} %shard_map.67.result_ref), custom_call_target="tpu_custom_call" | custom-call | tf_op jit(solution)/shard_map/pallas_call | solution.py:472
